TPU v7x, 128 devices: a whole 4x4x4 slice. The times are simulated.
128 devices in a mesh: row: 8 (over z_hi, y), col: 4 (over z_lo, core), depth: 4 (over x).
Axes of the slice: x: 4, y: 4, z: 4 (z_hi: 2, z_lo: 2; z = z_hi * 2 + z_lo), core: 2. Of those that a mesh axis runs over, the one named last changes fastest.
Arguments:
- tokens: bfloat16 [1024, 14848], P(('row', 'col'), 'depth'), may hold values from -6 to 6
- w_up: bfloat16 [14848, 32768], P('depth', ('row', 'col')), may hold values from -0.046875 to 0.046875
- grad_hidden: bfloat16 [1024, 32768], P('depth', ('row', 'col')), may hold values from -6 to 6
Outputs:
- hidden_act: bfloat16 [1024, 32768], P('depth', ('row', 'col'))
- input_grad: bfloat16 [1024, 14848], P(('row', 'col'), 'depth')
- weight_grad: bfloat16 [14848, 32768], P('depth', ('row', 'col'))
All inputs are finite; a program needn't handle non-finite values.
Results may differ from a plain program's by a relative error of at most 0.0049.
Values may be sent and summed in bfloat16 or wider, within the bound.
No kernel may reach another device: no remote copies, remote signals or barrier semaphores. Data moves between devices by JAX's collectives and lax.ppermute only.
A program may use at most 128 MiB of HBM per device.

v0:
```python
import jax
import jax.numpy as jnp
from jax import lax
from jax.sharding import PartitionSpec as P

root_half = 0.7071067811865476
norm_density = 0.3989422804014327


def gelu_value(values):
    return 0.5 * values * (1.0 + lax.erf(values * root_half))


def gelu_slope(values):
    return 0.5 * (1.0 + lax.erf(values * root_half)) + values * norm_density * jnp.exp(
        -0.5 * values * values
    )


def shards(tokens, w_up, grad_hidden):
    gathered = lax.all_gather(tokens, ("row", "col"), axis=0, tiled=True)
    partial_value = jnp.dot(gathered, w_up, preferred_element_type=jnp.float32)
    share_rows = grad_hidden.shape[0]
    pre_act = lax.psum(partial_value, "depth")
    grad_full = lax.all_gather(grad_hidden, "depth", axis=0, tiled=True)
    grad_pre = (grad_full.astype(jnp.float32) * gelu_slope(pre_act)).astype(jnp.bfloat16)
    own_part = lax.dynamic_slice_in_dim(
        pre_act, lax.axis_index("depth") * share_rows, share_rows, 0
    )
    hidden_act = gelu_value(own_part).astype(jnp.bfloat16)
    weight_grad = lax.dot_general(
        gathered, grad_pre, (((0,), (0,)), ((), ())), preferred_element_type=jnp.float32
    ).astype(jnp.bfloat16)
    input_grad = lax.psum_scatter(
        lax.dot_general(
            grad_pre, w_up, (((1,), (1,)), ((), ())), preferred_element_type=jnp.float32
        ),
        ("row", "col"),
        scatter_dimension=0,
        tiled=True,
    )
    return (hidden_act, input_grad.astype(jnp.bfloat16), weight_grad)


def solution(mesh):
    placed = (P(("row", "col"), "depth"), P("depth", ("row", "col")), P("depth", ("row", "col")))
    return jax.shard_map(
        shards,
        mesh=mesh,
        in_specs=placed,
        out_specs=(
            P("depth", ("row", "col")),
            P(("row", "col"), "depth"),
            P("depth", ("row", "col")),
        ),
        check_vma=False,
    )
```

profile of v0, /device:TPU:1, one launch (start us, length us, event | category | flops | bytes accessed | tf_op | source)
XLA Modules:
  0.0 398.2 jit_solution(11103624478340269830)
XLA Ops:
  7.2 0.0 all-gather.3.cloned.1.call-start
  7.2 0.7 all-gather.3.cloned.1.call-update
  7.9 0.0 all-gather.5.cloned.1.call-start
  7.9 0.7 all-gather.5.cloned.1.call-update
  8.6 0.0 all-reduce.2.cloned.1.call-start
  8.7 70.2 %all-gather.3.cloned.1.call-done = bf16[1024,3712]{1,0:T(8,128)(2,1)} async-done(((bf16[32,3712]{1,0:T(8,128)(2,1)}), bf16[1024,3712]{1,0:T(8,128)(2,1)}) %all-gather.3.cloned.1.call-update) | async-done | bytes 7602192 | tf_op jit(solution)/shard_map/all_gather | solution.py:21
  78.9 14.1 %fusion.5 = f32[1024,1024]{1,0:T(8,128)} fusion(bf16[1024,3712]{1,0:T(8,128)(2,1)} %all-gather.3.cloned.1.call-done, bf16[3712,1024]{1,0:T(8,128)(2,1)} %param.4), kind=kOutput, calls=%fused_computation.8 | convolution fusion | flops 7784628224 | bytes 19398656 | tf_op jit(solution)/shard_map/dot_general | solution.py:22
  93.0 0.0 all-reduce.2.cloned.1.call-update
  93.0 0.0 reduce-scatter.2.cloned.1.call-start
  93.0 17.3 %all-gather.5.cloned.1.call-done = bf16[1024,1024]{1,0:T(8,128)(2,1)} async-done(((bf16[256,1024]{1,0:T(8,128)(2,1)}), bf16[1024,1024]{1,0:T(8,128)(2,1)}) %all-gather.5.cloned.1.call-update) | async-done | bytes 2097168 | tf_op jit(solution)/shard_map/all_gather | solution.py:25
  110.4 95.8 %all-reduce.2.cloned.1.call-done = f32[1024,1024]{1,0:T(8,128)} async-done(((f32[1024,1024]{1,0:T(8,128)}), f32[1024,1024]{1,0:T(8,128)}) %all-reduce.2.cloned.1.call-update) | async-done | bytes 4194320 | tf_op jit(solution)/shard_map/psum | solution.py:24
  206.1 0.0 copy-start
  206.1 3.9 fusion.4
  210.0 1.1 copy-done
  211.2 11.1 %fusion.6 = f32[1024,3712]{1,0:T(8,128)} fusion(bf16[1024,1024]{1,0:T(8,128)(2,1)S(1)} %fusion.4, bf16[3712,1024]{1,0:T(8,128)(2,1)S(1)} %copy-done), kind=kOutput, calls=%fused_computation.9 | convolution fusion | flops 7784628224 | bytes 24903680 | tf_op jit(solution)/shard_map/dot_general | solution.py:35
  222.3 0.0 reduce-scatter.2.cloned.1.call-update
  222.4 13.8 %convert_bitcast_fusion = bf16[3712,1024]{0,1:T(8,128)(2,1)} fusion(bf16[1024,1024]{1,0:T(8,128)(2,1)S(1)} %fusion.4, bf16[1024,3712]{1,0:T(8,128)(2,1)} %all-gather.3.cloned.1.call-done), kind=kOutput, calls=%fused_computation | convolution fusion | flops 7788429312 | bytes 17301504 | tf_op jit(solution)/shard_map/dot_general | solution.py:31
  236.1 10.5 %copy.6 = bf16[3712,1024]{1,0:T(8,128)(2,1)} copy(bf16[3712,1024]{0,1:T(8,128)(2,1)} %convert_bitcast_fusion) | data formatting | bytes 15204352
  246.7 2.2 multiply_convert_fusion
  248.9 141.0 %reduce-scatter.2.cloned.1.call-done = f32[32,3712]{1,0:T(8,128)} async-done(((f32[1024,3712]{1,0:T(8,128)}), f32[32,3712]{1,0:T(8,128)}) %reduce-scatter.2.cloned.1.call-update) | async-done | bytes 475152 | tf_op jit(solution)/shard_map/reduce_scatter | solution.py:34
  389.9 1.7 convert_element_type.21
Async XLA Ops:
  7.2 71.7 %all-gather.3.cloned.1.call-start = ((), (), s32[]{:S(2)}) async-start(), calls=%async_computation.1 | async-start | bytes 7839744 | tf_op jit(solution)/shard_map/all_gather | solution.py:21
  7.9 102.5 %all-gather.5.cloned.1.call-start = ((), (), s32[]{:S(2)}) async-start(), calls=%async_computation.3 | async-start | bytes 2621440 | tf_op jit(solution)/shard_map/all_gather | solution.py:25
  8.6 197.5 %all-reduce.2.cloned.1.call-start = ((), (), s32[]{:S(2)}) async-start(), calls=%async_computation.2 | async-start | bytes 8388608 | tf_op jit(solution)/shard_map/psum | solution.py:24
  93.0 296.9 %reduce-scatter.2.cloned.1.call-start = ((), (), s32[]{:S(2)}) async-start(), calls=%async_computation.4 | async-start | bytes 15679488 | tf_op jit(solution)/shard_map/reduce_scatter | solution.py:34
  206.1 5.0 %copy-start = (bf16[3712,1024]{1,0:T(8,128)(2,1)S(1)}, bf16[3712,1024]{1,0:T(8,128)(2,1)}, u32[]{:S(2)}) copy-start(bf16[3712,1024]{1,0:T(8,128)(2,1)} %param.4) | copy-start | bytes 22806532
Sparse Core Ops, SparseCore 0:
  9.7 69.1 all-gather.2
  80.6 29.7 all-gather.4
  113.3 92.7 all-reduce.1
  222.5 167.4 reduce-scatter.1
where the time goes:
time: 402 us; the launch traced here: 398 us
  waiting for transfers between devices  326 us (81%)
  matrix products  39 us (10%)
  between operations  13.8 us (3%)
  local copies, waits for them, and re-layouts  11.7 us (3%)
  other arithmetic  7.84 us (2%)
    reduce_scatter x1, waiting for transfers between devices, shards(): lax.psum_scatter(lax.dot_general(grad_pre, w_up, (((1,), (1,)), ((), ()))...  141 us
    psum x1, waiting for transfers between devices, shards(): pre_act = lax.psum(partial_value, 'depth')  95.8 us
    all_gather x1, waiting for transfers between devices, shards(): gathered = lax.all_gather(tokens, ('row', 'col'), axis=0, tiled=True)  70.2 us
    all_gather x1, waiting for transfers between devices, shards(): grad_full = lax.all_gather(grad_hidden, 'depth', axis=0, tiled=True)  17.3 us
    dot_general x1, matrix products, shards(): partial_value = jnp.dot(gathered, w_up, preferred_element_type=jnp.float32)  14.1 us
    dot_general x1, matrix products, shards(): lax.dot_general(gathered, grad_pre, (((0,), (0,)), ((), ())), preferred_e...  13.8 us
    unnamed x3, local copies, waits for them, and re-layouts  11.7 us
    dot_general x1, matrix products, shards(): lax.dot_general(grad_pre, w_up, (((1,), (1,)), ((), ())), preferred_eleme...  11.1 us
  transfers between devices with their start and end apart: 4, of which 4 were waited for; matrix products, arithmetic and copies ran while one was open for 10% of the time, Pallas kernels for 0%

commit v1 on v0

v1 whole, which is shorter than its diff:
```python
import jax
import jax.numpy as jnp
from jax import lax
from jax.sharding import PartitionSpec as P

root_half = 0.7071067811865476
norm_density = 0.3989422804014327
PLANE = ("row", "col")
f32, bf16 = jnp.float32, jnp.bfloat16


def spot(z, y, core):
    return ((z // 2) * 4 + y) * 4 + (z % 2) * 2 + core


def plane_pairs(leg, way):
    pairs = []
    for z in range(4):
        for y in range(4):
            for core in range(2):
                on_y = (leg == "first") == (core == 0)
                to = ((z, (y + way) % 4) if on_y else ((z + way) % 4, y)) + (core,)
                pairs.append((spot(z, y, core), spot(*to)))
    return pairs


def move(block, leg, way):
    if leg == "depth":
        return lax.ppermute(block, "depth", [(i, (i + way) % 4) for i in range(4)])
    return lax.ppermute(block, PLANE, plane_pairs(leg, way))


def swap(block):
    return lax.ppermute(
        block,
        PLANE,
        [(spot(z, y, c), spot(z, y, 1 - c)) for z in range(4) for y in range(4) for c in range(2)],
    )


def pick(stack, at):
    return lax.dynamic_index_in_dim(stack, at, 0, keepdims=False)


def gather4(block, leg, at):
    half = block.shape[0] // 2
    below, above = move(block, leg, 1), move(block, leg, -1)
    far_low, far_high = move(below[:half], leg, 1), move(above[half:], leg, -1)
    whole = jnp.zeros((4,) + block.shape, block.dtype)
    for shift, part in ((0, block), (3, below), (1, above)):
        whole = lax.dynamic_update_slice_in_dim(whole, part[None], (at + shift) % 4, 0)
    far = jnp.concatenate([far_low, far_high], 0)
    return lax.dynamic_update_slice_in_dim(whole, far[None], (at + 2) % 4, 0)


def scatter4(stack, leg, at):
    half = stack.shape[1] // 2
    far, up, down = (pick(stack, (at + shift) % 4) for shift in (2, 1, 3))
    low = move(far[:half].astype(bf16), leg, 1)
    high = move(far[half:].astype(bf16), leg, -1)
    up = jnp.concatenate([up[:half] + low.astype(f32), up[half:]], 0).astype(bf16)
    down = jnp.concatenate([down[:half], down[half:] + high.astype(f32)], 0).astype(bf16)
    from_below, from_above = move(up, leg, 1), move(down, leg, -1)
    return pick(stack, at) + from_below.astype(f32) + from_above.astype(f32)


def by_owner(rows):
    one = rows[0].reshape((2, 2, 2, 2) + rows.shape[3:])
    two = rows[1].reshape((2, 2, 2, 2) + rows.shape[3:])
    one = one.transpose(0, 2, 1, 3, 4, 5)
    two = two.transpose(2, 0, 1, 3, 4, 5)
    both = jnp.stack([one, two], 2)
    return both.reshape((4,) + both.shape[2:])


def from_owner(rows):
    both = rows.reshape((2, 2) + rows.shape[1:])
    one = both[:, :, 0].transpose(0, 2, 1, 3, 4, 5)
    two = both[:, :, 1].transpose(1, 2, 0, 3, 4, 5)
    return jnp.stack([one.reshape((4, 4) + one.shape[4:]), two.reshape((4, 4) + two.shape[4:])], 0)


def owner_order(rows):
    split = rows.reshape(2, 2, 2, -1, rows.shape[-1])
    return jnp.stack([split[:, :, 0].transpose(1, 0, 2, 3), split[:, :, 1]], 0)


def token_order(rows):
    both = jnp.stack([rows[0].transpose(1, 0, 2, 3), rows[1]], 2)
    return both.reshape(-1, rows.shape[-1])


def shards(tokens, w_up, grad_hidden):
    row, col, depth = lax.axis_index("row"), lax.axis_index("col"), lax.axis_index("depth")
    z, y, core = (row // 4) * 2 + col // 2, row % 4, col % 2
    first, second = jnp.where(core == 0, y, z), jnp.where(core == 0, z, y)
    share, width = tokens.shape
    hidden = w_up.shape[1]

    own = gather4(gather4(tokens, "first", first), "second", second)
    other = swap(own)
    every = jnp.zeros((2,) + own.shape, own.dtype)
    every = lax.dynamic_update_slice_in_dim(every, own[None], core, 0)
    every = lax.dynamic_update_slice_in_dim(every, other[None], 1 - core, 0)
    flat = every.reshape(-1, width)

    partial_value = jnp.dot(flat, w_up, preferred_element_type=f32)
    owned = by_owner(partial_value.reshape(2, 4, 4, share, hidden))
    pre_act = scatter4(owned.reshape(4, -1, hidden), "depth", depth).reshape(owned.shape[1:])

    edge = lax.erf(pre_act * root_half)
    hidden_act = token_order((0.5 * pre_act * (1.0 + edge)).astype(bf16))
    slope = 0.5 * (1.0 + edge) + pre_act * norm_density * jnp.exp(-0.5 * pre_act * pre_act)
    grad_own = (owner_order(grad_hidden).astype(f32) * slope).astype(bf16)
    grads = gather4(grad_own.reshape(-1, hidden), "depth", depth)
    grads = from_owner(grads.reshape((4,) + grad_own.shape)).reshape(2, -1, hidden)

    def back(rows):
        return lax.dot_general(rows, w_up, (((1,), (1,)), ((), ())), preferred_element_type=f32)

    theirs = swap(back(pick(grads, 1 - core)).astype(bf16))
    ours = (back(pick(grads, core)) + theirs.astype(f32)).reshape(4, -1, width)
    line = scatter4(ours, "second", second).reshape(4, share, width)
    input_grad = scatter4(line, "first", first).astype(bf16)
    weight_grad = lax.dot_general(
        flat, grads.reshape(-1, hidden), (((0,), (0,)), ((), ())), preferred_element_type=f32
    ).astype(bf16)
    return hidden_act, input_grad, weight_grad


def solution(mesh):
    placed = (P(PLANE, "depth"), P("depth", PLANE), P("depth", PLANE))
    return jax.shard_map(
        shards,
        mesh=mesh,
        in_specs=placed,
        out_specs=(P("depth", PLANE), P(PLANE, "depth"), P("depth", PLANE)),
        check_vma=False,
    )
```

time: 402 us -> 201 us (0.50)
  waiting for transfers between devices: 326 us -> 82.6 us
  starting transfers between devices: 0.16 us -> 44.3 us
  local copies, waits for them, and re-layouts: 11.7 us -> 27.2 us
  between operations: 13.8 us -> 1.29 us
  matrix products: 39 us -> 29.6 us
  other arithmetic: 7.84 us -> 12.8 us
    reduce_scatter x1 -> x0, waiting for transfers between devices: 141 us -> none  [shards(): lax.psum_scatter(lax.dot_general(grad_pre, w_up, (((1,), (1,)), ((), ()))...]
    psum x1 -> x0, waiting for transfers between devices: 95.8 us -> none  [shards(): pre_act = lax.psum(partial_value, 'depth')]
    all_gather x2 -> x0, waiting for transfers between devices: 87.5 us -> none  [the longest x1 70.2 us: shards(): gathered = lax.all_gather(tokens, ('row', 'col'), axis=0, tiled=True)]
    ppermute x0 -> x26, waiting for transfers between devices: none -> 82.6 us  [the longest x16 40.6 us: move(): return lax.ppermute(block, PLANE, plane_pairs(leg, way))]
    ppermute x0 -> x26, starting transfers between devices: none -> 44.3 us  [the longest x16 25.6 us: move(): return lax.ppermute(block, PLANE, plane_pairs(leg, way))]
    dynamic_update_slice x0 -> x11, local copies, waits for them, and re-layouts: none -> 9.63 us  [the longest x9 4.16 us: gather4(): lax.dynamic_update_slice_in_dim(whole, part[None], (at + shift) % 4, 0)]
    dot_general x3 -> x4, matrix products: 39 us -> 29.6 us  [the longest x2 11.1 us: back(): lax.dot_general(rows, w_up, (((1,), (1,)), ((), ())), preferred_element_t...]
    slice x0 -> x12, local copies, waits for them, and re-layouts: none -> 4.78 us  [the longest x3 2.88 us: scatter4(): up[half:]]
  transfers between devices with their start and end apart: 4 -> 26, of which waited for: 4 -> 18; matrix products, arithmetic and copies ran while one was open for 10% -> 14% of each run, Pallas kernels for 0% -> 0%
where the time goes in v1:
time: 201 us; the launch traced here: 198 us
  waiting for transfers between devices  82.6 us (41%)
  starting transfers between devices  44.3 us (22%)
  matrix products  29.6 us (15%)
  local copies, waits for them, and re-layouts  27.2 us (14%)
  other arithmetic  12.8 us (6%)
    ppermute x16, waiting for transfers between devices, move(): return lax.ppermute(block, PLANE, plane_pairs(leg, way))  40.6 us
    ppermute x8, waiting for transfers between devices, move(): return lax.ppermute(block, 'depth', [(i, (i + way) % 4) for i in range(4)])  32.7 us
    ppermute x16, starting transfers between devices, move(): return lax.ppermute(block, PLANE, plane_pairs(leg, way))  25.6 us
    dot_general x2, matrix products, back(): lax.dot_general(rows, w_up, (((1,), (1,)), ((), ())), preferred_element_t...  11.1 us
    dot_general x1, matrix products, shards(): lax.dot_general(flat, grads.reshape(-1, hidden), (((0,), (0,)), ((), ()))...  10.2 us
    ppermute x2, starting transfers between devices, swap(): lax.ppermute(block, PLANE, [(spot(z, y, c), spot(z, y, 1 - c)) for z in r...  9.96 us
    ppermute x2, waiting for transfers between devices, swap(): lax.ppermute(block, PLANE, [(spot(z, y, c), spot(z, y, 1 - c)) for z in r...  9.33 us
    ppermute x8, starting transfers between devices, move(): return lax.ppermute(block, 'depth', [(i, (i + way) % 4) for i in range(4)])  8.74 us
  transfers between devices with their start and end apart: 26, of which 18 were waited for; matrix products, arithmetic and copies ran while one was open for 14% of the time, Pallas kernels for 0%

profile of v1, /device:TPU:1, one launch (start us, length us, event | category | flops | bytes accessed | tf_op | source)
XLA Modules:
  0.0 197.8 jit_solution(243081159550057113)
XLA Ops:
  0.6 2.5 %collective-permute-start = (bf16[32,3712]{1,0:T(8,128)(2,1)}, bf16[32,3712]{1,0:T(8,128)(2,1)S(1)}, u32[]{:S(2)}, u32[]{:S(2)}) collective-permute-start(bf16[32,3712]{1,0:T(8,128)(2,1)} %param.3), channel_id=1, source_target_pairs={{0,16},{4,12},{16,32},{20,28},{32,48},{36,44},{48,0},{52,60},{8,24... | collective-permute-start | bytes 712712 | tf_op jit(solution)/shard_map/ppermute | solution.py:30
  8.9 3.3 %collective-permute-start.3 = (bf16[16,3712]{1,0:T(8,128)(2,1)S(1)}, bf16[16,3712]{1,0:T(8,128)(2,1)S(1)}, u32[]{:S(2)}, u32[]{:S(2)}) collective-permute-start(bf16[16,3712]{1,0:T(8,128)(2,1)S(1)} %slice.199), channel_id=1, source_target_pairs={{0,48},{4,76},{16,0},{20,92},{32,16},{36,108},{48,32},{52,124},{8,... | collective-permute-start | bytes 356360 | tf_op jit(solution)/shard_map/ppermute | solution.py:30
  14.0 3.1 %collective-permute-done.2 = bf16[16,3712]{1,0:T(8,128)(2,1)S(1)} collective-permute-done((bf16[16,3712]{1,0:T(8,128)(2,1)S(1)}, bf16[16,3712]{1,0:T(8,128)(2,1)S(1)}, u32[]{:S(2)}, u32[]{:S(2)}) %collective-permute-start.2) | collective-permute-done | bytes 118816 | tf_op jit(solution)/shard_map/ppermute | solution.py:30
  17.1 2.8 %collective-permute-start.5 = (bf16[4,32,3712]{2,1,0:T(8,128)(2,1)S(1)}, bf16[4,32,3712]{2,1,0:T(8,128)(2,1)S(1)}, u32[]{:S(2)}, u32[]{:S(2)}) collective-permute-start(bf16[4,32,3712]{2,1,0:T(8,128)(2,1)S(1)} %fusion.39), channel_id=1, source_target_pairs={{0,72},{4,52},{16,88},{20,4},{32,104},{36,20},{48,120},{52,36},{8,... | collective-permute-start | bytes 2850824 | tf_op jit(solution)/shard_map/ppermute | solution.py:30
  23.2 7.5 %collective-permute-done.5 = bf16[4,32,3712]{2,1,0:T(8,128)(2,1)S(1)} collective-permute-done((bf16[4,32,3712]{2,1,0:T(8,128)(2,1)S(1)}, bf16[4,32,3712]{2,1,0:T(8,128)(2,1)S(1)}, u32[]{:S(2)}, u32[]{:S(2)}) %collective-permute-start.5) | collective-permute-done | bytes 950304 | tf_op jit(solution)/shard_map/ppermute | solution.py:30
  30.7 3.5 %collective-permute-start.7 = (bf16[2,32,3712]{2,1,0:T(8,128)(2,1)S(1)}, bf16[2,32,3712]{2,1,0:T(8,128)(2,1)S(1)}, u32[]{:S(2)}, u32[]{:S(2)}) collective-permute-start(bf16[2,32,3712]{2,1,0:T(8,128)(2,1)S(1)} %slice.201), channel_id=1, source_target_pairs={{0,72},{4,52},{16,88},{20,4},{32,104},{36,20},{48,120},{52,36},{8,... | collective-permute-start | bytes 1425416 | tf_op jit(solution)/shard_map/ppermute | solution.py:30
  36.3 3.5 %collective-permute-done.7 = bf16[2,32,3712]{2,1,0:T(8,128)(2,1)S(1)} collective-permute-done((bf16[2,32,3712]{2,1,0:T(8,128)(2,1)S(1)}, bf16[2,32,3712]{2,1,0:T(8,128)(2,1)S(1)}, u32[]{:S(2)}, u32[]{:S(2)}) %collective-permute-start.7) | collective-permute-done | bytes 475168 | tf_op jit(solution)/shard_map/ppermute | solution.py:30
  39.8 3.5 %collective-permute-done.6 = bf16[2,32,3712]{2,1,0:T(8,128)(2,1)S(1)} collective-permute-done((bf16[2,32,3712]{2,1,0:T(8,128)(2,1)S(1)}, bf16[2,32,3712]{2,1,0:T(8,128)(2,1)S(1)}, u32[]{:S(2)}, u32[]{:S(2)}) %collective-permute-start.6) | collective-permute-done | bytes 475168 | tf_op jit(solution)/shard_map/ppermute | solution.py:30
  44.3 5.1 %collective-permute-start.8 = (bf16[4,4,32,3712]{3,2,1,0:T(8,128)(2,1)}, bf16[4,4,32,3712]{3,2,1,0:T(8,128)(2,1)}, u32[]{:S(2)}, u32[]{:S(2)}) collective-permute-start(bf16[4,4,32,3712]{3,2,1,0:T(8,128)(2,1)} %fusion.23), channel_id=1, source_target_pairs={{0,4},{4,0},{16,20},{20,16},{32,36},{36,32},{48,52},{52,48},{8,12}... | collective-permute-start | bytes 11403272 | tf_op jit(solution)/shard_map/ppermute | solution.py:34
  50.1 2.8 %bitcast_dynamic-update-slice_fusion.1 = bf16[2,4,4,32,3712]{4,3,2,1,0:T(8,128)(2,1)S(1)} fusion(bf16[2,4,4,32,3712]{4,3,2,1,0:T(8,128)(2,1)S(1)} %broadcast_in_dim.51, s32[]{:T(128)S(6)} %select_n.178, bf16[4,4,32,3712]{3,2,1,0:T(8,128)(2,1)} %fusion.23), kind=kLoop, calls=%fused_computation.5 | loop fusion | bytes 7602180 | tf_op jit(solution)/shard_map/dynamic_update_slice | solution.py:103
  53.0 3.0 %collective-permute-done.8 = bf16[4,4,32,3712]{3,2,1,0:T(8,128)(2,1)} collective-permute-done((bf16[4,4,32,3712]{3,2,1,0:T(8,128)(2,1)}, bf16[4,4,32,3712]{3,2,1,0:T(8,128)(2,1)}, u32[]{:S(2)}, u32[]{:S(2)}) %collective-permute-start.8) | collective-permute-done | bytes 3801120 | tf_op jit(solution)/shard_map/ppermute | solution.py:34
  55.9 2.7 %bitcast_dynamic-update-slice_fusion = bf16[2,4,4,32,3712]{4,3,2,1,0:T(8,128)(2,1)S(1)} fusion(bf16[2,4,4,32,3712]{4,3,2,1,0:T(8,128)(2,1)S(1)} %bitcast_dynamic-update-slice_fusion.1, s32[]{:T(128)S(6)} %select_n.179, bf16[4,4,32,3712]{3,2,1,0:T(8,128)(2,1)} %collective-permute-done.8), kind=kLoop, calls=%fused_computation.4 | loop fusion | bytes 7602180 | tf_op jit(solution)/shard_map/dynamic_update_slice | solution.py:104
  58.6 8.3 %fusion.50 = f32[1024,1024]{1,0:T(8,128)S(1)} fusion(bf16[1024,3712]{1,0:T(8,128)(2,1)S(1)} %bitcast.189, bf16[3712,1024]{1,0:T(8,128)(2,1)S(1)} %bitcast.212), kind=kOutput, calls=%fused_computation.109 | convolution fusion | flops 7784628224 | bytes 19398656 | tf_op jit(solution)/shard_map/dot_general | solution.py:107
  74.5 4.8 %collective-permute-done.9 = bf16[128,1024]{1,0:T(8,128)(2,1)S(1)} collective-permute-done((bf16[128,1024]{1,0:T(8,128)(2,1)S(1)}, bf16[128,1024]{1,0:T(8,128)(2,1)S(1)}, u32[]{:S(2)}, u32[]{:S(2)}) %collective-permute-start.9) | collective-permute-done | bytes 262176 | tf_op jit(solution)/shard_map/ppermute | solution.py:29
  83.3 9.6 %collective-permute-done.12 = bf16[256,1024]{1,0:T(8,128)(2,1)S(1)} collective-permute-done((bf16[256,1024]{1,0:T(8,128)(2,1)S(1)}, bf16[256,1024]{1,0:T(8,128)(2,1)S(1)}, u32[]{:S(2)}, u32[]{:S(2)}) %collective-permute-start.12) | collective-permute-done | bytes 524320 | tf_op jit(solution)/shard_map/ppermute | solution.py:29
  92.9 3.1 %collective-permute-done.10 = bf16[256,1024]{1,0:T(8,128)(2,1)S(1)} collective-permute-done((bf16[256,1024]{1,0:T(8,128)(2,1)S(1)}, bf16[256,1024]{1,0:T(8,128)(2,1)S(1)}, u32[]{:S(2)}, u32[]{:S(2)}) %collective-permute-start.10) | collective-permute-done | bytes 524320 | tf_op jit(solution)/shard_map/ppermute | solution.py:29
  96.0 2.7 %fusion.8 = (bf16[256,1024]{1,0:T(8,128)(2,1)S(1)}, bf16[256,1024]{1,0:T(8,128)(2,1)}) fusion(bf16[2,2,2,32,1024]{4,3,2,1,0:T(8,128)(2,1)S(1)} %pad_maximum_fusion.6, bf16[256,1024]{1,0:T(8,128)(2,1)S(1)} %collective-permute-done.12, bf16[256,1024]{1,0:T(8,128)(2,1)S(1)} %collective-permute-done.10, f32[4,256,1024]{2,1,0:T(8,128)} %bitcast.183, s32[]{:T(128)S(6)} %select_n.180), kind=kLoop, calls=%fused_computation.23 | loop fusion | flops 4718592 | bytes 3670020 | tf_op jit(solution)/shard_map/convert_element_type | solution.py:114
  100.5 8.9 %collective-permute-done.14 = bf16[256,1024]{1,0:T(8,128)(2,1)S(1)} collective-permute-done((bf16[256,1024]{1,0:T(8,128)(2,1)S(1)}, bf16[256,1024]{1,0:T(8,128)(2,1)S(1)}, u32[]{:S(2)}, u32[]{:S(2)}) %collective-permute-start.14) | collective-permute-done | bytes 524320 | tf_op jit(solution)/shard_map/ppermute | solution.py:29
  111.6 3.6 %collective-permute-done.16 = bf16[128,1024]{1,0:T(8,128)(2,1)S(1)} collective-permute-done((bf16[128,1024]{1,0:T(8,128)(2,1)S(1)}, bf16[128,1024]{1,0:T(8,128)(2,1)S(1)}, u32[]{:S(2)}, u32[]{:S(2)}) %collective-permute-start.16) | collective-permute-done | bytes 262176 | tf_op jit(solution)/shard_map/ppermute | solution.py:29
  115.2 2.7 %collective-permute-done.15 = bf16[128,1024]{1,0:T(8,128)(2,1)S(1)} collective-permute-done((bf16[128,1024]{1,0:T(8,128)(2,1)S(1)}, bf16[128,1024]{1,0:T(8,128)(2,1)S(1)}, u32[]{:S(2)}, u32[]{:S(2)}) %collective-permute-start.15) | collective-permute-done | bytes 262176 | tf_op jit(solution)/shard_map/ppermute | solution.py:29
  120.7 4.7 %convolution_convert_fusion = bf16[512,3712]{1,0:T(8,128)(2,1)S(1)} fusion(bf16[3712,1024]{1,0:T(8,128)(2,1)S(1)} %bitcast.214, s32[]{:T(128)S(6)} %select_n.179, bf16[1,512,1024]{2,1,0:T(8,128)(2,1)S(1)} %bitcast.200, bf16[1,512,1024]{2,1,0:T(8,128)(2,1)S(1)} %bitcast.203), kind=kOutput, calls=%fused_computation.2 | convolution fusion | flops 3894738944 | bytes 13500420 | tf_op jit(solution)/shard_map/dot_general | solution.py:119
  125.4 4.9 %collective-permute-start.17 = (bf16[512,3712]{1,0:T(8,128)(2,1)S(1)}, bf16[512,3712]{1,0:T(8,128)(2,1)}, u32[]{:S(2)}, u32[]{:S(2)}) collective-permute-start(bf16[512,3712]{1,0:T(8,128)(2,1)S(1)} %convolution_convert_fusion), channel_id=1, source_target_pairs={{0,4},{4,0},{16,20},{20,16},{32,36},{36,32},{48,52},{52,48},{8,12}... | collective-permute-start | bytes 11403272 | tf_op jit(solution)/shard_map/ppermute | solution.py:34
  130.3 6.4 %collective-permute-done.17 = bf16[512,3712]{1,0:T(8,128)(2,1)} collective-permute-done((bf16[512,3712]{1,0:T(8,128)(2,1)S(1)}, bf16[512,3712]{1,0:T(8,128)(2,1)}, u32[]{:S(2)}, u32[]{:S(2)}) %collective-permute-start.17) | collective-permute-done | bytes 3801120 | tf_op jit(solution)/shard_map/ppermute | solution.py:34
  136.6 6.4 %convert_add_fusion = f32[512,3712]{1,0:T(8,128)S(1)} fusion(bf16[512,3712]{1,0:T(8,128)(2,1)} %collective-permute-done.17, bf16[3712,1024]{1,0:T(8,128)(2,1)S(1)} %bitcast.214, s32[]{:T(128)S(6)} %select_n.178, bf16[1,512,1024]{2,1,0:T(8,128)(2,1)S(1)} %bitcast.201, bf16[1,512,1024]{2,1,0:T(8,128)(2,1)S(1)} %bitcast.204), kind=kOutput, calls=%fused_computation.1 | convolution fusion | flops 3896639488 | bytes 21102596 | tf_op jit(solution)/shard_map/dot_general | solution.py:119
  143.0 3.1 %copy-done.2 = f32[512,3712]{1,0:T(8,128)} copy-done((f32[512,3712]{1,0:T(8,128)}, f32[512,3712]{1,0:T(8,128)S(1)}, u32[]{:S(2)}) %copy-start.2) | copy-done | bytes 7602200
  146.4 2.7 %collective-permute-start.20 = (bf16[64,3712]{1,0:T(8,128)(2,1)S(1)}, bf16[64,3712]{1,0:T(8,128)(2,1)S(1)}, u32[]{:S(2)}, u32[]{:S(2)}) collective-permute-start(bf16[64,3712]{1,0:T(8,128)(2,1)S(1)} %get-tuple-element.22), channel_id=1, source_target_pairs={{0,72},{4,52},{16,88},{20,4},{32,104},{36,20},{48,120},{52,36},{8,... | collective-permute-start | bytes 1425416 | tf_op jit(solution)/shard_map/ppermute | solution.py:30
  150.7 4.8 %collective-permute-done.18 = bf16[64,3712]{1,0:T(8,128)(2,1)S(1)} collective-permute-done((bf16[64,3712]{1,0:T(8,128)(2,1)S(1)}, bf16[64,3712]{1,0:T(8,128)(2,1)S(1)}, u32[]{:S(2)}, u32[]{:S(2)}) %collective-permute-start.18) | collective-permute-done | bytes 475168 | tf_op jit(solution)/shard_map/ppermute | solution.py:30
  163.8 7.7 %collective-permute-done.21 = bf16[128,3712]{1,0:T(8,128)(2,1)} collective-permute-done((bf16[128,3712]{1,0:T(8,128)(2,1)}, bf16[128,3712]{1,0:T(8,128)(2,1)}, u32[]{:S(2)}, u32[]{:S(2)}) %collective-permute-start.21) | collective-permute-done | bytes 950304 | tf_op jit(solution)/shard_map/ppermute | solution.py:30
  171.4 4.4 %collective-permute-done.19 = bf16[128,3712]{1,0:T(8,128)(2,1)} collective-permute-done((bf16[128,3712]{1,0:T(8,128)(2,1)}, bf16[128,3712]{1,0:T(8,128)(2,1)}, u32[]{:S(2)}, u32[]{:S(2)}) %collective-permute-start.19) | collective-permute-done | bytes 950304 | tf_op jit(solution)/shard_map/ppermute | solution.py:30
  178.4 2.7 %collective-permute-start.24 = (bf16[16,3712]{1,0:T(8,128)(2,1)S(1)}, bf16[16,3712]{1,0:T(8,128)(2,1)S(1)}, u32[]{:S(2)}, u32[]{:S(2)}) collective-permute-start(bf16[16,3712]{1,0:T(8,128)(2,1)S(1)} %get-tuple-element.30), channel_id=1, source_target_pairs={{0,48},{4,76},{16,0},{20,92},{32,16},{36,108},{48,32},{52,124},{8,... | collective-permute-start | bytes 356360 | tf_op jit(solution)/shard_map/ppermute | solution.py:30
  183.3 3.0 %collective-permute-start.25 = (bf16[32,3712]{1,0:T(8,128)(2,1)S(1)}, bf16[32,3712]{1,0:T(8,128)(2,1)S(1)}, u32[]{:S(2)}, u32[]{:S(2)}) collective-permute-start(bf16[32,3712]{1,0:T(8,128)(2,1)S(1)} %pad_maximum_fusion.8), channel_id=1, source_target_pairs={{0,48},{4,76},{16,0},{20,92},{32,16},{36,108},{48,32},{52,124},{8,... | collective-permute-start | bytes 712712 | tf_op jit(solution)/shard_map/ppermute | solution.py:30
  186.8 10.2 %bitcast_convert_fusion = bf16[3712,1024]{1,0:T(8,128)(2,1)} fusion(bf16[2,4,4,32,3712]{4,3,2,1,0:T(8,128)(2,1)S(1)} %bitcast.191, bf16[1,4,4,32,1024]{4,3,2,1,0:T(8,128)(2,1)S(1)} %bitcast.205, bf16[1,4,4,32,1024]{4,3,2,1,0:T(8,128)(2,1)S(1)} %bitcast.202), kind=kOutput, calls=%fused_computation | convolution fusion | flops 7789477888 | bytes 17301504 | tf_op jit(solution)/shard_map/dot_general | solution.py:125
  (113 shorter events, 48.8 us)
Async XLA Ops:
  0.6 11.5 %collective-permute-start = (bf16[32,3712]{1,0:T(8,128)(2,1)}, bf16[32,3712]{1,0:T(8,128)(2,1)S(1)}, u32[]{:S(2)}, u32[]{:S(2)}) collective-permute-start(bf16[32,3712]{1,0:T(8,128)(2,1)} %param.3), channel_id=1, source_target_pairs={{0,16},{4,12},{16,32},{20,28},{32,48},{36,44},{48,0},{52,60},{8,24... | collective-permute-start | bytes 712712 | tf_op jit(solution)/shard_map/ppermute | solution.py:30
  3.2 5.7 %collective-permute-start.1 = (bf16[32,3712]{1,0:T(8,128)(2,1)}, bf16[32,3712]{1,0:T(8,128)(2,1)S(1)}, u32[]{:S(2)}, u32[]{:S(2)}) collective-permute-start(bf16[32,3712]{1,0:T(8,128)(2,1)} %param.3), channel_id=1, source_target_pairs={{0,48},{4,76},{16,0},{20,92},{32,16},{36,108},{48,32},{52,124},{8,... | collective-permute-start | bytes 712712 | tf_op jit(solution)/shard_map/ppermute | solution.py:30
  8.9 5.1 %collective-permute-start.3 = (bf16[16,3712]{1,0:T(8,128)(2,1)S(1)}, bf16[16,3712]{1,0:T(8,128)(2,1)S(1)}, u32[]{:S(2)}, u32[]{:S(2)}) collective-permute-start(bf16[16,3712]{1,0:T(8,128)(2,1)S(1)} %slice.199), channel_id=1, source_target_pairs={{0,48},{4,76},{16,0},{20,92},{32,16},{36,108},{48,32},{52,124},{8,... | collective-permute-start | bytes 356360 | tf_op jit(solution)/shard_map/ppermute | solution.py:30
  12.1 5.0 %collective-permute-start.2 = (bf16[16,3712]{1,0:T(8,128)(2,1)S(1)}, bf16[16,3712]{1,0:T(8,128)(2,1)S(1)}, u32[]{:S(2)}, u32[]{:S(2)}) collective-permute-start(bf16[16,3712]{1,0:T(8,128)(2,1)S(1)} %slice.198), channel_id=1, source_target_pairs={{0,16},{4,12},{16,32},{20,28},{32,48},{36,44},{48,0},{52,60},{8,24... | collective-permute-start | bytes 356360 | tf_op jit(solution)/shard_map/ppermute | solution.py:30
  17.1 13.5 %collective-permute-start.5 = (bf16[4,32,3712]{2,1,0:T(8,128)(2,1)S(1)}, bf16[4,32,3712]{2,1,0:T(8,128)(2,1)S(1)}, u32[]{:S(2)}, u32[]{:S(2)}) collective-permute-start(bf16[4,32,3712]{2,1,0:T(8,128)(2,1)S(1)} %fusion.39), channel_id=1, source_target_pairs={{0,72},{4,52},{16,88},{20,4},{32,104},{36,20},{48,120},{52,36},{8,... | collective-permute-start | bytes 2850824 | tf_op jit(solution)/shard_map/ppermute | solution.py:30
  19.9 14.2 %collective-permute-start.4 = (bf16[4,32,3712]{2,1,0:T(8,128)(2,1)S(1)}, bf16[4,32,3712]{2,1,0:T(8,128)(2,1)S(1)}, u32[]{:S(2)}, u32[]{:S(2)}) collective-permute-start(bf16[4,32,3712]{2,1,0:T(8,128)(2,1)S(1)} %fusion.39), channel_id=1, source_target_pairs={{0,8},{4,20},{16,24},{20,36},{32,40},{36,52},{48,56},{52,4},{8,64}... | collective-permute-start | bytes 2850824 | tf_op jit(solution)/shard_map/ppermute | solution.py:30
  30.7 9.1 %collective-permute-start.7 = (bf16[2,32,3712]{2,1,0:T(8,128)(2,1)S(1)}, bf16[2,32,3712]{2,1,0:T(8,128)(2,1)S(1)}, u32[]{:S(2)}, u32[]{:S(2)}) collective-permute-start(bf16[2,32,3712]{2,1,0:T(8,128)(2,1)S(1)} %slice.201), channel_id=1, source_target_pairs={{0,72},{4,52},{16,88},{20,4},{32,104},{36,20},{48,120},{52,36},{8,... | collective-permute-start | bytes 1425416 | tf_op jit(solution)/shard_map/ppermute | solution.py:30
  34.2 9.1 %collective-permute-start.6 = (bf16[2,32,3712]{2,1,0:T(8,128)(2,1)S(1)}, bf16[2,32,3712]{2,1,0:T(8,128)(2,1)S(1)}, u32[]{:S(2)}, u32[]{:S(2)}) collective-permute-start(bf16[2,32,3712]{2,1,0:T(8,128)(2,1)S(1)} %slice.200), channel_id=1, source_target_pairs={{0,8},{4,20},{16,24},{20,36},{32,40},{36,52},{48,56},{52,4},{8,64}... | collective-permute-start | bytes 1425416 | tf_op jit(solution)/shard_map/ppermute | solution.py:30
  44.3 11.7 %collective-permute-start.8 = (bf16[4,4,32,3712]{3,2,1,0:T(8,128)(2,1)}, bf16[4,4,32,3712]{3,2,1,0:T(8,128)(2,1)}, u32[]{:S(2)}, u32[]{:S(2)}) collective-permute-start(bf16[4,4,32,3712]{3,2,1,0:T(8,128)(2,1)} %fusion.23), channel_id=1, source_target_pairs={{0,4},{4,0},{16,20},{20,16},{32,36},{36,32},{48,52},{52,48},{8,12}... | collective-permute-start | bytes 11403272 | tf_op jit(solution)/shard_map/ppermute | solution.py:34
  70.4 8.8 %collective-permute-start.9 = (bf16[128,1024]{1,0:T(8,128)(2,1)S(1)}, bf16[128,1024]{1,0:T(8,128)(2,1)S(1)}, u32[]{:S(2)}, u32[]{:S(2)}) collective-permute-start(bf16[128,1024]{1,0:T(8,128)(2,1)S(1)} %get-tuple-element.27), channel_id=1, source_target_pairs={{0,1},{1,2},{2,3},{3,0},{4,5},{5,6},{6,7},{7,4},{8,9},{9,10},{10,1... | collective-permute-start | bytes 786440 | tf_op jit(solution)/shard_map/ppermute | solution.py:29
  71.7 7.5 %collective-permute-start.11 = (bf16[128,1024]{1,0:T(8,128)(2,1)S(1)}, bf16[128,1024]{1,0:T(8,128)(2,1)S(1)}, u32[]{:S(2)}, u32[]{:S(2)}) collective-permute-start(bf16[128,1024]{1,0:T(8,128)(2,1)S(1)} %get-tuple-element.28), channel_id=1, source_target_pairs={{0,3},{1,0},{2,1},{3,2},{4,7},{5,4},{6,5},{7,6},{8,11},{9,8},{10,9... | collective-permute-start | bytes 786440 | tf_op jit(solution)/shard_map/ppermute | solution.py:29
  80.6 12.3 %collective-permute-start.12 = (bf16[256,1024]{1,0:T(8,128)(2,1)S(1)}, bf16[256,1024]{1,0:T(8,128)(2,1)S(1)}, u32[]{:S(2)}, u32[]{:S(2)}) collective-permute-start(bf16[256,1024]{1,0:T(8,128)(2,1)S(1)} %pad_maximum_fusion.4), channel_id=1, source_target_pairs={{0,3},{1,0},{2,1},{3,2},{4,7},{5,4},{6,5},{7,6},{8,11},{9,8},{10,9... | collective-permute-start | bytes 1572872 | tf_op jit(solution)/shard_map/ppermute | solution.py:29
  83.1 12.9 %collective-permute-start.10 = (bf16[256,1024]{1,0:T(8,128)(2,1)S(1)}, bf16[256,1024]{1,0:T(8,128)(2,1)S(1)}, u32[]{:S(2)}, u32[]{:S(2)}) collective-permute-start(bf16[256,1024]{1,0:T(8,128)(2,1)S(1)} %pad_maximum_fusion.3), channel_id=1, source_target_pairs={{0,1},{1,2},{2,3},{3,0},{4,5},{5,6},{6,7},{7,4},{8,9},{9,10},{10,1... | collective-permute-start | bytes 1572872 | tf_op jit(solution)/shard_map/ppermute | solution.py:29
  98.7 10.7 %collective-permute-start.14 = (bf16[256,1024]{1,0:T(8,128)(2,1)S(1)}, bf16[256,1024]{1,0:T(8,128)(2,1)S(1)}, u32[]{:S(2)}, u32[]{:S(2)}) collective-permute-start(bf16[256,1024]{1,0:T(8,128)(2,1)S(1)} %get-tuple-element.7), channel_id=1, source_target_pairs={{0,3},{1,0},{2,1},{3,2},{4,7},{5,4},{6,5},{7,6},{8,11},{9,8},{10,9... | collective-permute-start | bytes 1572872 | tf_op jit(solution)/shard_map/ppermute | solution.py:29
  98.9 12.3 %collective-permute-start.13 = (bf16[256,1024]{1,0:T(8,128)(2,1)S(1)}, bf16[256,1024]{1,0:T(8,128)(2,1)S(1)}, u32[]{:S(2)}, u32[]{:S(2)}) collective-permute-start(bf16[256,1024]{1,0:T(8,128)(2,1)S(1)} %get-tuple-element.7), channel_id=1, source_target_pairs={{0,1},{1,2},{2,3},{3,0},{4,5},{5,6},{6,7},{7,4},{8,9},{9,10},{10,1... | collective-permute-start | bytes 1572872 | tf_op jit(solution)/shard_map/ppermute | solution.py:29
  100.2 18.3 %slice-start.4 = ((s8[7602176]{0:T(1024)(128)(4,1)}), s8[4194304]{0:T(1024)(128)(4,1)S(1)}, s32[]{:S(2)}) async-start(s8[7602176]{0:T(1024)(128)(4,1)} %bitcast.213), calls=%async_computation.4 | async-start | bytes 8388608
  109.4 5.8 %collective-permute-start.16 = (bf16[128,1024]{1,0:T(8,128)(2,1)S(1)}, bf16[128,1024]{1,0:T(8,128)(2,1)S(1)}, u32[]{:S(2)}, u32[]{:S(2)}) collective-permute-start(bf16[128,1024]{1,0:T(8,128)(2,1)S(1)} %slice.211), channel_id=1, source_target_pairs={{0,3},{1,0},{2,1},{3,2},{4,7},{5,4},{6,5},{7,6},{8,11},{9,8},{10,9... | collective-permute-start | bytes 786440 | tf_op jit(solution)/shard_map/ppermute | solution.py:29
  111.2 6.7 %collective-permute-start.15 = (bf16[128,1024]{1,0:T(8,128)(2,1)S(1)}, bf16[128,1024]{1,0:T(8,128)(2,1)S(1)}, u32[]{:S(2)}, u32[]{:S(2)}) collective-permute-start(bf16[128,1024]{1,0:T(8,128)(2,1)S(1)} %slice.210), channel_id=1, source_target_pairs={{0,1},{1,2},{2,3},{3,0},{4,5},{5,6},{6,7},{7,4},{8,9},{9,10},{10,1... | collective-permute-start | bytes 786440 | tf_op jit(solution)/shard_map/ppermute | solution.py:29
  118.3 18.3 %copy-start.3 = (bf16[2,2,2,2,32,1024]{5,4,3,2,1,0:T(8,128)(2,1)}, bf16[2,2,2,2,32,1024]{5,4,3,2,1,0:T(8,128)(2,1)S(1)}, u32[]{:S(2)}) copy-start(bf16[2,2,2,2,32,1024]{5,4,3,2,1,0:T(8,128)(2,1)S(1)} %copy.23) | copy-start | bytes 3145732
  125.4 11.2 %collective-permute-start.17 = (bf16[512,3712]{1,0:T(8,128)(2,1)S(1)}, bf16[512,3712]{1,0:T(8,128)(2,1)}, u32[]{:S(2)}, u32[]{:S(2)}) collective-permute-start(bf16[512,3712]{1,0:T(8,128)(2,1)S(1)} %convolution_convert_fusion), channel_id=1, source_target_pairs={{0,4},{4,0},{16,20},{20,16},{32,36},{36,32},{48,52},{52,48},{8,12}... | collective-permute-start | bytes 11403272 | tf_op jit(solution)/shard_map/ppermute | solution.py:34
  146.3 9.1 %collective-permute-start.18 = (bf16[64,3712]{1,0:T(8,128)(2,1)S(1)}, bf16[64,3712]{1,0:T(8,128)(2,1)S(1)}, u32[]{:S(2)}, u32[]{:S(2)}) collective-permute-start(bf16[64,3712]{1,0:T(8,128)(2,1)S(1)} %get-tuple-element.21), channel_id=1, source_target_pairs={{0,8},{4,20},{16,24},{20,36},{32,40},{36,52},{48,56},{52,4},{8,64}... | collective-permute-start | bytes 1425416 | tf_op jit(solution)/shard_map/ppermute | solution.py:30
  146.4 9.0 %collective-permute-start.20 = (bf16[64,3712]{1,0:T(8,128)(2,1)S(1)}, bf16[64,3712]{1,0:T(8,128)(2,1)S(1)}, u32[]{:S(2)}, u32[]{:S(2)}) collective-permute-start(bf16[64,3712]{1,0:T(8,128)(2,1)S(1)} %get-tuple-element.22), channel_id=1, source_target_pairs={{0,72},{4,52},{16,88},{20,4},{32,104},{36,20},{48,120},{52,36},{8,... | collective-permute-start | bytes 1425416 | tf_op jit(solution)/shard_map/ppermute | solution.py:30
  158.1 13.4 %collective-permute-start.21 = (bf16[128,3712]{1,0:T(8,128)(2,1)}, bf16[128,3712]{1,0:T(8,128)(2,1)}, u32[]{:S(2)}, u32[]{:S(2)}) collective-permute-start(bf16[128,3712]{1,0:T(8,128)(2,1)} %pad_maximum_fusion.2), channel_id=1, source_target_pairs={{0,72},{4,52},{16,88},{20,4},{32,104},{36,20},{48,120},{52,36},{8,... | collective-permute-start | bytes 2850824 | tf_op jit(solution)/shard_map/ppermute | solution.py:30
  160.4 26.3 %slice-start = ((s8[7602176]{0:T(1024)(128)(4,1)}), s8[3407872]{0:T(1024)(128)(4,1)S(1)}, s32[]{:S(2)}) async-start(s8[7602176]{0:T(1024)(128)(4,1)} %bitcast.190), calls=%async_computation | async-start | bytes 6815744
  161.4 14.4 %collective-permute-start.19 = (bf16[128,3712]{1,0:T(8,128)(2,1)}, bf16[128,3712]{1,0:T(8,128)(2,1)}, u32[]{:S(2)}, u32[]{:S(2)}) collective-permute-start(bf16[128,3712]{1,0:T(8,128)(2,1)} %pad_maximum_fusion.1), channel_id=1, source_target_pairs={{0,8},{4,20},{16,24},{20,36},{32,40},{36,52},{48,56},{52,4},{8,64}... | collective-permute-start | bytes 2850824 | tf_op jit(solution)/shard_map/ppermute | solution.py:30
  163.8 23.0 %slice-start.1 = ((s8[7602176]{0:T(1024)(128)(4,1)}), s8[4194304]{0:T(1024)(128)(4,1)S(1)}, s32[]{:S(2)}) async-start(s8[7602176]{0:T(1024)(128)(4,1)} %bitcast.190), calls=%async_computation.1 | async-start | bytes 8388608
  163.8 23.0 %copy-start.4 = (bf16[2,2,2,2,32,1024]{5,4,3,2,1,0:T(8,128)(2,1)S(1)}, bf16[2,2,2,2,32,1024]{5,4,3,2,1,0:T(8,128)(2,1)}, u32[]{:S(2)}) copy-start(bf16[2,2,2,2,32,1024]{5,4,3,2,1,0:T(8,128)(2,1)} %copy-done.3) | copy-start | bytes 3145732
  163.8 23.0 %copy-start.6 = (bf16[2,2,2,2,32,1024]{5,4,3,2,1,0:T(8,128)(2,1)S(1)}, bf16[2,2,2,2,32,1024]{5,4,3,2,1,0:T(8,128)(2,1)}, u32[]{:S(2)}) copy-start(bf16[2,2,2,2,32,1024]{5,4,3,2,1,0:T(8,128)(2,1)} %copy-done.5) | copy-start | bytes 3145732
  178.3 5.0 %collective-permute-start.22 = (bf16[16,3712]{1,0:T(8,128)(2,1)S(1)}, bf16[16,3712]{1,0:T(8,128)(2,1)S(1)}, u32[]{:S(2)}, u32[]{:S(2)}) collective-permute-start(bf16[16,3712]{1,0:T(8,128)(2,1)S(1)} %get-tuple-element.29), channel_id=1, source_target_pairs={{0,16},{4,12},{16,32},{20,28},{32,48},{36,44},{48,0},{52,60},{8,24... | collective-permute-start | bytes 356360 | tf_op jit(solution)/shard_map/ppermute | solution.py:30
  178.4 4.9 %collective-permute-start.24 = (bf16[16,3712]{1,0:T(8,128)(2,1)S(1)}, bf16[16,3712]{1,0:T(8,128)(2,1)S(1)}, u32[]{:S(2)}, u32[]{:S(2)}) collective-permute-start(bf16[16,3712]{1,0:T(8,128)(2,1)S(1)} %get-tuple-element.30), channel_id=1, source_target_pairs={{0,48},{4,76},{16,0},{20,92},{32,16},{36,108},{48,32},{52,124},{8,... | collective-permute-start | bytes 356360 | tf_op jit(solution)/shard_map/ppermute | solution.py:30
  183.3 13.7 %collective-permute-start.25 = (bf16[32,3712]{1,0:T(8,128)(2,1)S(1)}, bf16[32,3712]{1,0:T(8,128)(2,1)S(1)}, u32[]{:S(2)}, u32[]{:S(2)}) collective-permute-start(bf16[32,3712]{1,0:T(8,128)(2,1)S(1)} %pad_maximum_fusion.8), channel_id=1, source_target_pairs={{0,48},{4,76},{16,0},{20,92},{32,16},{36,108},{48,32},{52,124},{8,... | collective-permute-start | bytes 712712 | tf_op jit(solution)/shard_map/ppermute | solution.py:30
  186.4 10.6 %collective-permute-start.23 = (bf16[32,3712]{1,0:T(8,128)(2,1)S(1)}, bf16[32,3712]{1,0:T(8,128)(2,1)S(1)}, u32[]{:S(2)}, u32[]{:S(2)}) collective-permute-start(bf16[32,3712]{1,0:T(8,128)(2,1)S(1)} %pad_maximum_fusion.7), channel_id=1, source_target_pairs={{0,16},{4,12},{16,32},{20,28},{32,48},{36,44},{48,0},{52,60},{8,24... | collective-permute-start | bytes 712712 | tf_op jit(solution)/shard_map/ppermute | solution.py:30
  (8 other events, 63.4 us)
